TPU v7x, 256 devices: a whole 4x4x8 slice. The times are simulated.
256 devices in a mesh: pp: 8 (over y_hi, x), dp: 8 (over z), tp: 4 (over y_lo, core).
Axes of the slice: x: 4, y: 4 (y_hi: 2, y_lo: 2; y = y_hi * 2 + y_lo), z: 8, core: 2. Of those that a mesh axis runs over, the one named last changes fastest.
Arguments:
- hidden: bfloat16 [256, 128, 8192], P(('pp', 'dp'), None, 'tp'), may hold values from -6 to 6
- positions: int32 [256, 8], P(('pp', 'dp')), may hold values from 0 to 127, as said below
- image_tokens: int32 [256], P(('pp', 'dp')), may hold values from 1 to 8, as said below
- groups: int32 [256, 1], P(('pp', 'dp')), may hold values from 0 to 7; in each aligned block of 4 rows (0 to 3, 4 to 7, ...) at most 2 rows name the same one
- latents: bfloat16 [256, 8, 1536], P(('pp', 'dp')), may hold values from -6 to 6
- out_grad: bfloat16 [256, 8, 1536], P(('pp', 'dp'), None, 'tp'), may hold values from -6 to 6
- w_conn: bfloat16 [1536, 8192], P(None, 'tp'), may hold values from -0.0625 to 0.0625
- w_mod: bfloat16 [1536, 3, 1536], P(('pp', 'dp'), None, 'tp'), may hold values from -0.15625 to 0.15625
- w_up: bfloat16 [8, 1536, 6144], P('dp', 'pp', 'tp'), may hold values from -0.15625 to 0.15625
- w_down: bfloat16 [8, 1536, 6144], P('dp', 'pp', 'tp'), may hold values from -0.078125 to 0.078125
Outputs:
- generated: bfloat16 [256, 8, 1536], P(('pp', 'dp'), None, 'tp')
- row_grad: bfloat16 [256, 8, 8192], P(('pp', 'dp'), None, 'tp')
- conn_grad: float32 [1536, 8192], P(('pp', 'dp'), 'tp')
Inputs may be any that keep to these rules, and one draw needn't show every extreme that they name: Each sample's 8 positions are distinct and increasing. `image_tokens`: the first sample of each aligned block of 4 samples uses all 8. `groups`: within the rows of one device (aligned blocks of 4) no group is named more than 2 times.
All inputs are finite; a program needn't handle non-finite values.
Results may differ from a plain program's by a relative error of at most 0.034.
Values may be sent and summed in bfloat16 or wider, within the bound.
A program may use at most 128 MiB of HBM per device.

v0:
```python
import jax
import jax.numpy as jnp
from jax import lax
from jax.sharding import PartitionSpec as P

CAP = 2


tanh_coef = 0.7978845608028654
cubic_term = 0.044715


def gelu_pair(preact):
    inner_arg = tanh_coef * (preact + cubic_term * preact * preact * preact)
    tanh_value = jnp.tanh(inner_arg)
    gelu_value = 0.5 * preact * (1.0 + tanh_value)
    gelu_slope = 0.5 * (1.0 + tanh_value) + 0.5 * preact * (
        1.0 - tanh_value * tanh_value
    ) * tanh_coef * (1.0 + 3.0 * cubic_term * preact * preact)
    return (gelu_value, gelu_slope)


def normalize(latent):
    average = jnp.mean(latent, axis=-1, keepdims=True)
    centered = latent - average
    variance = jnp.mean(centered * centered, axis=-1, keepdims=True)
    return centered / jnp.sqrt(variance + 1e-06)


def to_slots(onehot, source):
    flattened = source.reshape(source.shape[0], -1)
    packed = jnp.dot(onehot, flattened, preferred_element_type=jnp.float32)
    return packed.astype(source.dtype).reshape((onehot.shape[0],) + source.shape[1:])


def from_slots(onehot, source):
    flattened = source.reshape(source.shape[0], -1)
    spread = jnp.dot(onehot.T, flattened, preferred_element_type=jnp.float32)
    return spread.astype(source.dtype).reshape((onehot.shape[1],) + source.shape[1:])


def local(hidden, positions, image_tokens, groups, latents, out_grad, w_conn, w_mod, w_up, w_down):
    local_samples, image_len = positions.shape
    row_depth = hidden.shape[2]
    cond_width = latents.shape[2]
    share_width = out_grad.shape[2]
    group_total = lax.axis_size("dp")
    slot_total = group_total * CAP
    slot_rows = slot_total * image_len
    tp_index = lax.axis_index("tp")
    data_shards = lax.axis_size("pp") * lax.axis_size("dp")
    picked = jnp.take_along_axis(hidden, positions[:, :, None], axis=1)
    target = groups[:, 0]
    sample_order = jnp.arange(local_samples)
    earlier = (target[None, :] == target[:, None]) & (sample_order[None, :] < sample_order[:, None])
    rank_index = jnp.sum(earlier.astype(jnp.int32), axis=1)
    slot_index = target * CAP + rank_index
    onehot = (jnp.arange(slot_total)[:, None] == slot_index[None, :]).astype(jnp.bfloat16)
    valid_mask = (jnp.arange(image_len)[None, :] < image_tokens[:, None]).astype(jnp.bfloat16)
    full_mod = lax.all_gather(w_mod, ("pp", "dp"), axis=0, tiled=True)
    full_up, full_down = (
        lax.all_gather(w_up, "pp", axis=1, tiled=True),
        lax.all_gather(w_down, "pp", axis=1, tiled=True),
    )
    full_up = full_up[0]
    full_down = full_down[0]
    mod_matrix = full_mod.reshape(cond_width, 3 * share_width)

    def in_groups(source):
        return to_slots(onehot, source).reshape((group_total, CAP) + source.shape[1:])

    received = (
        lax.all_to_all(in_groups(picked), "dp", split_axis=0, concat_axis=0, tiled=True),
        lax.all_to_all(in_groups(latents), "dp", split_axis=0, concat_axis=0, tiled=True),
        lax.all_to_all(in_groups(out_grad), "dp", split_axis=0, concat_axis=0, tiled=True),
        lax.all_to_all(in_groups(valid_mask), "dp", split_axis=0, concat_axis=0, tiled=True),
    )
    got_rows = received[0].reshape(slot_rows, row_depth)
    cond_part = jnp.einsum("rd,cd->rc", got_rows, w_conn, preferred_element_type=jnp.float32)
    condition = lax.psum(cond_part.astype(jnp.bfloat16), "tp")
    live_mask = received[3].reshape(slot_rows, 1).astype(jnp.float32)
    latent = received[1].reshape(slot_rows, cond_width)
    modulation = jnp.dot(condition, mod_matrix, preferred_element_type=jnp.float32).reshape(
        slot_rows, 3, share_width
    )
    shift_part = modulation[:, 0]
    scale_part = modulation[:, 1]
    gate_part = modulation[:, 2]
    normed_full = normalize(latent.astype(jnp.float32))
    normed = lax.dynamic_slice_in_dim(normed_full, tp_index * share_width, share_width, 1)
    latent_part = lax.dynamic_slice_in_dim(latent, tp_index * share_width, share_width, 1).astype(
        jnp.float32
    )
    h_part = (normed * (1.0 + scale_part) + shift_part).astype(jnp.bfloat16)
    h_full = lax.all_gather(h_part, "tp", axis=1, tiled=True)
    preact = jnp.dot(h_full, full_up, preferred_element_type=jnp.float32)
    gelu_value, gelu_slope = gelu_pair(preact)
    activation = gelu_value.astype(jnp.bfloat16)
    ff_part = jnp.einsum("rf,cf->rc", activation, full_down, preferred_element_type=jnp.float32)
    ff_out = lax.psum_scatter(
        ff_part.astype(jnp.bfloat16), "tp", scatter_dimension=1, tiled=True
    ).astype(jnp.float32)
    cotangent = received[2].reshape(slot_rows, share_width).astype(jnp.float32)
    generated_part = (live_mask * (latent_part + gate_part * ff_out)).astype(jnp.bfloat16)
    d_out = (gate_part * cotangent).astype(jnp.bfloat16)
    d_full = lax.all_gather(d_out, "tp", axis=1, tiled=True)
    d_act = jnp.dot(d_full, full_down, preferred_element_type=jnp.float32)
    d_pre = (d_act * gelu_slope).astype(jnp.bfloat16)
    d_hin_part = jnp.einsum("rf,cf->rc", d_pre, full_up, preferred_element_type=jnp.float32)
    d_hin = lax.psum_scatter(
        d_hin_part.astype(jnp.bfloat16), "tp", scatter_dimension=1, tiled=True
    ).astype(jnp.float32)
    d_mod = jnp.stack([d_hin, d_hin * normed, cotangent * ff_out], axis=1).astype(jnp.bfloat16)
    d_cond_part = jnp.einsum(
        "rk,ck->rc",
        d_mod.reshape(slot_rows, 3 * share_width),
        mod_matrix,
        preferred_element_type=jnp.float32,
    )
    generated_part, d_cond_part = (generated_part, d_cond_part)
    d_cond = (
        live_mask * lax.psum(d_cond_part.astype(jnp.bfloat16), "tp").astype(jnp.float32)
    ).astype(jnp.bfloat16)
    grad_rows = jnp.dot(d_cond, w_conn, preferred_element_type=jnp.float32).astype(jnp.bfloat16)
    returned = (
        lax.all_to_all(
            grad_rows.reshape(group_total, CAP, image_len, row_depth),
            "dp",
            split_axis=0,
            concat_axis=0,
            tiled=True,
        ),
        lax.all_to_all(
            generated_part.reshape(group_total, CAP, image_len, share_width),
            "dp",
            split_axis=0,
            concat_axis=0,
            tiled=True,
        ),
    )
    grad_total = lax.psum_scatter(
        jnp.einsum("rc,rd->cd", d_cond, got_rows, preferred_element_type=jnp.float32),
        ("pp", "dp"),
        scatter_dimension=0,
        tiled=True,
    )
    row_out = from_slots(onehot, returned[0].reshape(slot_total, image_len, row_depth))
    generated_out = from_slots(onehot, returned[1].reshape(slot_total, image_len, share_width))
    conn_grad = grad_total / float(data_shards)
    return (generated_out, row_out, conn_grad)


def solution(mesh):
    placed = (
        P(("pp", "dp"), None, "tp"),
        P(("pp", "dp"), None),
        P(("pp", "dp")),
        P(("pp", "dp"), None),
        P(("pp", "dp"), None, None),
        P(("pp", "dp"), None, "tp"),
        P(None, "tp"),
        P(("pp", "dp"), None, "tp"),
        P("dp", "pp", "tp"),
        P("dp", "pp", "tp"),
    )
    return jax.shard_map(
        local,
        mesh=mesh,
        in_specs=placed,
        out_specs=(P(("pp", "dp"), None, "tp"), P(("pp", "dp"), None, "tp"), P(("pp", "dp"), "tp")),
        check_vma=False,
    )
```

profile of v0, /device:TPU:1, one launch (start us, length us, event | category | flops | bytes accessed | tf_op | source)
XLA Modules:
  0.0 1252.4 jit_solution(3027140882718966075)
XLA Ops:
  9.6 1.0 gather_fusion
  13.7 25.1 %all_to_all.30 = bf16[8,2,8,2048]{3,2,1,0:T(8,128)(2,1)S(1)} all-to-all(bf16[8,2,8,2048]{3,2,1,0:T(8,128)(2,1)S(1)} %bitcast.129), channel_id=1, replica_groups=mesh['pp'=8,'dp'=8,'tp'=4] {'dp'}, dimensions={0} | all-to-all | bytes 1048576 | tf_op jit(solution)/shard_map/all_to_all | solution.py:73
  38.8 5.7 convolution_convert_fusion.6
  47.3 3.5 all-to-all-start.1
  51.6 10.9 all-to-all-done.1
  62.5 3.4 all-to-all-start.4
  66.5 72.6 %all-gather.4.cloned.1.call-done = bf16[1536,3,384]{2,0,1:T(8,128)(2,1)} async-done(((bf16[24,3,384]{2,0,1:T(8,128)(2,1)}), bf16[1536,3,384]{2,0,1:T(8,128)(2,1)}) %all-gather.4.cloned.1.call-update) | async-done | bytes 3538960 | tf_op jit(solution)/shard_map/all_gather | solution.py:60
  139.1 6.1 copy.19
  145.2 4.2 fusion.8
  149.4 1.2 fusion.51
  150.6 12.0 all_gather.16
  162.7 7.0 all_gather.19
  169.7 54.9 %all-gather.6.cloned.1.call-done = bf16[1,1536,1536]{2,1,0:T(8,128)(2,1)} async-done(((bf16[1,192,1536]{2,1,0:T(8,128)(2,1)}), bf16[1,1536,1536]{2,1,0:T(8,128)(2,1)}) %all-gather.6.cloned.1.call-update) | async-done | bytes 4718608 | tf_op jit(solution)/shard_map/all_gather | solution.py:62
  224.6 4.0 fusion.6
  228.6 77.9 %all-gather.8.cloned.1.call-done = bf16[1,1536,1536]{2,1,0:T(8,128)(2,1)} async-done(((bf16[1,192,1536]{2,1,0:T(8,128)(2,1)}), bf16[1,1536,1536]{2,1,0:T(8,128)(2,1)}) %all-gather.8.cloned.1.call-update) | async-done | bytes 4718608 | tf_op jit(solution)/shard_map/all_gather | solution.py:63
  306.6 6.7 fusion.14
  314.3 4.2 fusion.17
  319.9 13.1 %all_to_all.31 = bf16[8,2,8]{2,1,0:T(2,128)(2,1)S(1)} all-to-all(bf16[8,2,8]{2,1,0:T(2,128)(2,1)S(1)} %bitcast.148), channel_id=1, replica_groups=mesh['pp'=8,'dp'=8,'tp'=4] {'dp'}, dimensions={0} | all-to-all | bytes 512 | tf_op jit(solution)/shard_map/all_to_all | solution.py:76
  333.5 1.0 copy.23
  334.5 22.6 %reduce-scatter.10.cloned.1.call-done = bf16[384,128]{1,0:T(8,128)(2,1)} async-done(((bf16[1536,128]{1,0:T(8,128)(2,1)}), bf16[384,128]{1,0:T(8,128)(2,1)}) %reduce-scatter.10.cloned.1.call-update) | async-done | bytes 98320
  357.2 1.0 copy.21
  358.2 1.7 fusion.60
  359.9 4.0 fusion.13
  364.2 42.6 %all-reduce.5.cloned.1.call-done = bf16[128,1536]{1,0:T(8,128)(2,1)} async-done(((bf16[128,1536]{1,0:T(8,128)(2,1)}), bf16[128,1536]{1,0:T(8,128)(2,1)}) %all-reduce.5.cloned.1.call-update) | async-done | bytes 393232 | tf_op jit(solution)/shard_map/psum | solution.py:122
  406.8 7.4 fusion.57
  414.2 6.9 all-to-all-start.3
  421.1 4.7 convolution_convert_fusion.5
  425.8 2.9 all-to-all-done.3
  428.6 3.8 all-to-all-start.5
  433.2 19.4 %all-to-all-done.5 = bf16[8,2,8,2048]{3,2,1,0:T(8,128)(2,1)S(1)} async-done(((bf16[8,2,8,2048]{3,2,1,0:T(8,128)(2,1)}), bf16[8,2,8,2048]{3,2,1,0:T(8,128)(2,1)S(1)}, u32[]{:S(2)}, u32[]{:S(2)}) %all-to-all-start.5) | async-done | bytes 524320 | tf_op jit(solution)/shard_map/all_to_all | solution.py:126
  454.0 789.4 %reduce-scatter.8.cloned.1.call-done = f32[24,2048]{1,0:T(8,128)} async-done(((f32[1536,2048]{1,0:T(8,128)}), f32[24,2048]{1,0:T(8,128)}) %reduce-scatter.8.cloned.1.call-update) | async-done | bytes 196624 | tf_op jit(solution)/shard_map/reduce_scatter | solution.py:141
  1243.4 1.6 broadcast_multiply_fusion
  (61 shorter events, 14.0 us)
Async XLA Ops:
  8.0 1.6 copy-start
  8.0 131.1 %all-gather.4.cloned.1.call-start = ((), (), s32[]{:S(2)}) async-start(), calls=%async_computation.10 | async-start | bytes 3594240 | tf_op jit(solution)/shard_map/all_gather | solution.py:60
  8.7 136.5 %all-reduce.3.cloned.1.call-start = ((), (), s32[]{:S(2)}) async-start(), calls=%async_computation.9 | async-start | bytes 786432 | tf_op jit(solution)/shard_map/psum | solution.py:80
  13.7 32.4 %copy-start.2 = (bf16[4,8,1536]{2,1,0:T(8,128)(2,1)S(1)}, bf16[4,8,1536]{2,1,0:T(8,128)(2,1)}, u32[]{:S(2)}) copy-start(bf16[4,8,1536]{2,1,0:T(8,128)(2,1)} %param.14) | copy-start | bytes 294916
  38.8 11.9 copy-start.3
  44.6 180.1 %all-gather.6.cloned.1.call-start = ((), (), s32[]{:S(2)}) async-start(), calls=%async_computation.11 | async-start | bytes 5308416 | tf_op jit(solution)/shard_map/all_gather | solution.py:62
  45.3 261.3 %all-gather.8.cloned.1.call-start = ((), (), s32[]{:S(2)}) async-start(), calls=%async_computation.12 | async-start | bytes 5308416 | tf_op jit(solution)/shard_map/all_gather | solution.py:63
  47.3 15.2 %all-to-all-start.1 = ((bf16[8,2,8,1536]{3,2,1,0:T(8,128)(2,1)}), bf16[8,2,8,1536]{3,2,1,0:T(8,128)(2,1)S(1)}, u32[]{:S(2)}, u32[]{:S(2)}) async-start(bf16[8,2,8,1536]{3,2,1,0:T(8,128)(2,1)} %bitcast.33), calls=%async_computation.1 | async-start | bytes 786432 | tf_op jit(solution)/shard_map/all_to_all | solution.py:74
  62.5 86.9 %all-to-all-start.4 = ((bf16[8,2,8,384]{3,2,1,0:T(8,128)(2,1)}), bf16[8,2,8,384]{3,2,1,0:T(8,128)(2,1)S(1)}, u32[]{:S(2)}, u32[]{:S(2)}) async-start(bf16[8,2,8,384]{3,2,1,0:T(8,128)(2,1)} %bitcast.49), calls=%async_computation.4 | async-start | bytes 196608 | tf_op jit(solution)/shard_map/all_to_all | solution.py:75
  65.9 267.7 %reduce-scatter.12.cloned.1.call-start = ((), (), s32[]{:S(2)}) async-start(), calls=%async_computation.16 | async-start | bytes 491520
  313.3 6.3 copy-start.4
  314.3 42.9 %reduce-scatter.10.cloned.1.call-start = ((), (), s32[]{:S(2)}) async-start(), calls=%async_computation.15 | async-start | bytes 491520
  319.5 87.2 %all-reduce.5.cloned.1.call-start = ((), (), s32[]{:S(2)}) async-start(), calls=%async_computation.13 | async-start | bytes 786432 | tf_op jit(solution)/shard_map/psum | solution.py:122
  363.9 879.4 %reduce-scatter.8.cloned.1.call-start = ((), (), s32[]{:S(2)}) async-start(), calls=%async_computation.14 | async-start | bytes 12779520 | tf_op jit(solution)/shard_map/reduce_scatter | solution.py:141
  414.2 6.9 copy-start.1
  414.2 14.4 %all-to-all-start.3 = ((bf16[8,2,8,384]{3,2,1,0:T(8,128)(2,1)}), bf16[8,2,8,384]{3,2,1,0:T(8,128)(2,1)S(1)}, u32[]{:S(2)}, u32[]{:S(2)}) async-start(bf16[8,2,8,384]{3,2,1,0:T(8,128)(2,1)} %bitcast.15), calls=%async_computation.3 | async-start | bytes 196608 | tf_op jit(solution)/shard_map/all_to_all | solution.py:133
  428.6 24.0 %all-to-all-start.5 = ((bf16[8,2,8,2048]{3,2,1,0:T(8,128)(2,1)}), bf16[8,2,8,2048]{3,2,1,0:T(8,128)(2,1)S(1)}, u32[]{:S(2)}, u32[]{:S(2)}) async-start(bf16[8,2,8,2048]{3,2,1,0:T(8,128)(2,1)} %bitcast.22), calls=%async_computation.5 | async-start | bytes 1048576 | tf_op jit(solution)/shard_map/all_to_all | solution.py:126
Sparse Core Ops, SparseCore 0:
  12.9 126.1 all-gather.3
  142.0 82.5 all-gather.5
  227.6 78.9 all-gather.7
  414.3 828.9 reduce-scatter.7
Sparse Core Ops, SparseCore 1:
  44.6 41.4 all-reduce.2
  314.3 19.1 reduce-scatter.11
  335.9 21.2 reduce-scatter.9
  364.0 42.7 all-reduce.4
where the time goes:
time: 1260 us; the launch traced here: 1250 us
  waiting for transfers between devices  1100 us (87%)
  blocking collectives  57.2 us (5%)
  matrix products  42.4 us (3%)
  starting transfers between devices  18 us (1%)
  between operations  15.7 us (1%)
  local copies, waits for them, and re-layouts  15.2 us (1%)
    reduce_scatter x1, waiting for transfers between devices, local(): lax.psum_scatter(jnp.einsum('rc,rd->cd', d_cond, got_rows, preferred_elem...  789 us
    all_gather x1, waiting for transfers between devices, local(): lax.all_gather(w_down, 'pp', axis=1, tiled=True)  77.9 us
    all_gather x1, waiting for transfers between devices, local(): full_mod = lax.all_gather(w_mod, ('pp', 'dp'), axis=0, tiled=True)  72.6 us
    all_gather x1, waiting for transfers between devices, local(): lax.all_gather(w_up, 'pp', axis=1, tiled=True)  54.9 us
    psum x1, waiting for transfers between devices, local(): lax.psum(d_cond_part.astype(jnp.bfloat16), 'tp').astype(jnp.float32)  42.6 us
    unnamed x10, waiting for transfers between devices  25.2 us
  transfers between devices with their start and end apart: 12, of which 10 were waited for; matrix products, arithmetic and copies ran while one was open for 3% of the time, Pallas kernels for 0%

commit v1 on v0

v1 whole, which is shorter than its diff:
```python
import functools

import jax
import jax.numpy as jnp
from jax import lax
from jax.experimental import pallas as pl
from jax.experimental.pallas import tpu as pltpu
from jax.sharding import PartitionSpec as P

MESH = pl.DeviceIdType.MESH
CAP = 2
F32 = jnp.float32
BF16 = jnp.bfloat16
tanh_coef = 0.7978845608028654
cubic_term = 0.044715


def gelu_pair(preact):
    inner_arg = tanh_coef * (preact + cubic_term * preact * preact * preact)
    tanh_value = jnp.tanh(inner_arg)
    gelu_value = 0.5 * preact * (1.0 + tanh_value)
    gelu_slope = 0.5 * (1.0 + tanh_value) + 0.5 * preact * (
        1.0 - tanh_value * tanh_value
    ) * tanh_coef * (1.0 + 3.0 * cubic_term * preact * preact)
    return (gelu_value, gelu_slope)


def dot_nn(a, b):
    return lax.dot_general(a, b, (((1,), (0,)), ((), ())), preferred_element_type=F32)


def dot_nt(a, b):
    return lax.dot_general(a, b, (((1,), (1,)), ((), ())), preferred_element_type=F32)


def kernel(
    groups, tokens, positions, hidden, latents, out_grad, w_conn, w_mod, w_up, w_down,
    gen_o, row_o, conn_o,
    hid, wc, wu, wd, wm, pick, pkg,
    cps, cpr, cbz, cz, mps, mrs,
    slot, hd, slope_s, ffs, rff, dhs, rdh, rets, ret,
    rdm, dcs, dcr, dcz, dch, cgs, rcg,
    lsem, ssem, rsem,
):
    p, z, t = lax.axis_index("pp"), lax.axis_index("dp"), lax.axis_index("tp")
    yh, x = p // 4, lax.rem(p, 4)
    m = yh * 4 + t
    rows = 32

    def zdev(d):
        return (p, lax.rem(z + d + 8, 8), t)

    def pdev(d):
        return (lax.rem(p + d, 8), z, t)

    def tdev(e):
        return (p, z, lax.rem(t + e, 4))

    def mdev(e):
        mm = lax.rem(m + e, 8)
        return ((mm // 4) * 4 + x, z, lax.rem(mm, 4))

    loc = []

    def load(src, dst):
        c = pltpu.make_async_copy(src, dst, lsem.at[len(loc)])
        c.start()
        loc.append(c)
        return c

    c_hid = load(hidden, hid)
    c_wc = [
        load(w_conn.at[pl.ds(512 * i, 512)], wc.at[pl.ds(512 * i, 512)]) for i in range(3)
    ]

    barrier = pltpu.get_barrier_semaphore()
    peers = [zdev(d) for d in range(1, 8)]
    peers += [pdev(d) for d in (1, 2, 3, 5, 6, 7)]
    peers += [mdev(e) for e in range(1, 8)]
    for dev in peers:
        pl.semaphore_signal(barrier, inc=1, device_id=dev, device_id_type=MESH)
    pl.semaphore_wait(barrier, len(peers))

    sent = []

    def send(src, dst, dev):
        k = len(sent)
        c = pltpu.make_async_remote_copy(
            src_ref=src, dst_ref=dst, send_sem=ssem.at[k], recv_sem=rsem.at[k],
            device_id=dev, device_id_type=MESH,
        )
        c.start()
        sent.append(c)
        return c

    def arrive(copies):
        for c in copies:
            c.wait_recv()

    wm[p] = w_mod[...]
    r_wm = [send(w_mod, wm.at[p], pdev(d)) for d in range(1, 8)]

    own_rows = pl.ds(pl.multiple_of(192 * p, 192), 192)

    def half(ref, which):
        return ref.at[0, :, pl.ds(pl.multiple_of(768 * which, 768), 768)]

    def spread(src, dst):
        out = []
        for d in range(1, 8):
            dev = pdev(d)
            out.append(send(half(src, dev[0] // 4), dst.at[own_rows], dev))
        return out

    c_wu = load(half(w_up, yh), wu.at[own_rows])
    c_wd = load(half(w_down, yh), wd.at[own_rows])
    r_wu = spread(w_up, wu)
    r_wd = spread(w_down, wd)

    seq_iota = lax.broadcasted_iota(jnp.int32, (8, 128), 1)
    row_iota = lax.broadcasted_iota(jnp.int32, (8, 128), 0)
    c_hid.wait()
    parts = []
    for s in range(4):
        at = jnp.zeros((8, 128), jnp.int32)
        for i in range(8):
            at = jnp.where(row_iota == i, positions[s, i], at)
        sel = jnp.where(seq_iota == at, 1.0, 0.0).astype(BF16)
        parts.append(dot_nn(sel, hid[s]))
    pick[...] = jnp.concatenate(parts, axis=0).astype(BF16)
    pkg[0] = pick[...]

    for i in range(3):
        c_wc[i].wait()
        part = dot_nt(pick[...], wc[pl.ds(512 * i, 512), :])
        cps[:, pl.ds(512 * i, 512)] = part.astype(BF16)
    r_cp = [send(cps, cpr.at[e - 1], tdev(e)) for e in range(1, 4)]

    lat = latents[...].astype(F32).reshape(rows, 1536)
    mean = jnp.mean(lat, axis=-1, keepdims=True)
    cent = lat - mean
    var = jnp.mean(cent * cent, axis=-1, keepdims=True)
    inv = 1.0 / jnp.sqrt(var + 1e-06)
    mine = pl.ds(pl.multiple_of(t * 384, 384), 384)
    lat_t = latents[:, :, mine].astype(F32).reshape(rows, 384)
    normed = (lat_t - mean) * inv
    cot = out_grad[...].astype(F32).reshape(rows, 384)

    gs = [groups[s, 0] for s in range(4)]
    places = []
    for s in range(4):
        rank = 0
        for q in range(s):
            rank = rank + jnp.where(gs[q] == gs[s], 1, 0)
        places.append(gs[s] * CAP + rank)
    big_r = lax.broadcasted_iota(jnp.int32, (128, rows), 0)
    big_c = lax.broadcasted_iota(jnp.int32, (128, rows), 1)
    place = jnp.zeros((128, rows), jnp.int32)
    for s in range(4):
        place = jnp.where(big_c // 8 == s, places[s], place)
    onehot = jnp.where(big_r == place * 8 + lax.rem(big_c, 8), 1.0, 0.0).astype(BF16)
    flip_r = lax.broadcasted_iota(jnp.int32, (rows, 128), 0)
    flip_c = lax.broadcasted_iota(jnp.int32, (rows, 128), 1)
    place_f = jnp.zeros((rows, 128), jnp.int32)
    for s in range(4):
        place_f = jnp.where(flip_r // 8 == s, places[s], place_f)
    onehot_f = jnp.where(flip_c == place_f * 8 + lax.rem(flip_r, 8), 1.0, 0.0).astype(BF16)
    one_r = lax.broadcasted_iota(jnp.int32, (rows, 384), 0)
    used = jnp.zeros((rows, 384), jnp.int32)
    for s in range(4):
        used = jnp.where(one_r // 8 == s, tokens[s], used)
    valid = jnp.where(lax.rem(one_r, 8) < used, 1.0, 0.0)

    arrive(r_cp)
    cond = cps[...].astype(F32)
    for e in range(3):
        cond = cond + cpr[e].astype(F32)
    cond = cond.astype(BF16).astype(F32).T
    gap = jnp.zeros((8, rows), F32)
    pieces = []
    for zz in range(8):
        for pp in range(8):
            pieces.append(cond[24 * (8 * pp + zz) : 24 * (8 * pp + zz) + 24])
            pieces.append(gap)
    cond = jnp.concatenate(pieces, axis=0).T.astype(BF16)
    for zz in range(8):
        cbz[zz] = cond[:, 256 * zz : 256 * zz + 256]
    r_cz = []
    for d in range(1, 8):
        dev = zdev(d)
        r_cz.append(send(cbz.at[dev[1]], cz.at[d], dev))
    cz[0] = cbz[z]

    arrive(r_wm)
    wmod = wm[...].reshape(256, 1152)
    r_mr = []
    arrive(r_cz)
    pooled = cz[...].reshape(256, 256)
    mod_all = dot_nn(pooled, wmod).astype(BF16).reshape(8, rows, 1152)
    mps[...] = mod_all
    for d in (4, 3, 5, 2, 6, 1, 7):
        r_mr.append(send(mps.at[d], mrs.at[d], zdev(-d)))
    mod = mps[0].astype(F32)
    arrive(r_mr)
    for d in range(1, 8):
        mod = mod + mrs[d].astype(F32)
    shift, scale, gate = mod[:, :384], mod[:, 384:768], mod[:, 768:]

    h_in = (normed * (1.0 + scale) + shift).astype(BF16)
    d_out = (gate * cot).astype(BF16)
    packed = dot_nn(onehot, jnp.concatenate([h_in, d_out], axis=1)).astype(BF16)
    slot[...] = packed.reshape(8, 16, 768)
    r_sl = []
    for d in range(1, 8):
        dev = zdev(d)
        r_sl.append(send(slot.at[dev[1]], hd.at[m, pl.ds(16 * d, 16)], dev))
    hd[m, pl.ds(0, 16)] = slot[z]
    arrive(r_sl)
    r_h = [send(hd.at[m, :, pl.ds(0, 384)], hd.at[m, :, pl.ds(0, 384)], mdev(e)) for e in range(1, 8)]
    r_d = [send(hd.at[m, :, pl.ds(384, 384)], hd.at[m, :, pl.ds(384, 384)], mdev(e)) for e in range(1, 8)]
    r_pk = [send(pick, pkg.at[d], zdev(d)) for d in range(1, 8)]

    c_wu.wait()
    arrive(r_wu)
    arrive(r_h)

    def both(k, lo):
        return jnp.concatenate([hd[k, :, lo : lo + 384], hd[4 + k, :, lo : lo + 384]], axis=0)

    pre = dot_nn(both(0, 0), wu[0:384, :])
    for k in range(1, 4):
        pre = pre + dot_nn(both(k, 0), wu[384 * k : 384 * k + 384, :])
    value, slope = gelu_pair(pre)
    act = value.astype(BF16)
    slope_s[...] = slope
    c_wd.wait()
    arrive(r_wd)
    for k in range(4):
        ff = dot_nt(act, wd[384 * k : 384 * k + 384, :]).astype(BF16)
        ffs[k] = ff[:128]
        ffs[4 + k] = ff[128:]
    r_ff = []
    for e in range(1, 8):
        r_ff.append(send(ffs.at[lax.rem(m + e, 8)], rff.at[e - 1], mdev(e)))
    arrive(r_d)
    d_act = dot_nn(both(0, 384), wd[0:384, :])
    for k in range(1, 4):
        d_act = d_act + dot_nn(both(k, 384), wd[384 * k : 384 * k + 384, :])
    d_pre = (d_act * slope_s[...]).astype(BF16)
    for k in range(4):
        dh = dot_nt(d_pre, wu[384 * k : 384 * k + 384, :]).astype(BF16)
        dhs[k] = dh[:128]
        dhs[4 + k] = dh[128:]
    r_dh = []
    for e in range(1, 8):
        r_dh.append(send(dhs.at[lax.rem(m + e, 8)], rdh.at[e - 1], mdev(e)))
    arrive(r_ff)
    total = ffs[m].astype(F32)
    for e in range(7):
        total = total + rff[e].astype(F32)
    rets[:, :, pl.ds(0, 384)] = total.astype(BF16).reshape(8, 16, 384)
    arrive(r_dh)
    total = dhs[m].astype(F32)
    for e in range(7):
        total = total + rdh[e].astype(F32)
    rets[:, :, pl.ds(384, 384)] = total.astype(BF16).reshape(8, 16, 384)
    r_rt = [send(rets.at[d], ret.at[z], zdev(-d)) for d in range(1, 8)]
    ret[z] = rets[0]
    arrive(r_rt)
    home = dot_nn(onehot_f, ret[...].reshape(128, 768))
    ff_out, d_hin = home[:, :384], home[:, 384:]
    gen_o[...] = (valid * (lat_t + gate * ff_out)).reshape(4, 8, 384).astype(BF16)
    d_mod = jnp.concatenate(
        [valid * d_hin, valid * (d_hin * normed), valid * (cot * ff_out)], axis=1
    )
    rdm[0] = d_mod.astype(BF16)
    r_dm = [send(rdm.at[0], rdm.at[d], zdev(d)) for d in (4, 3, 5, 2, 6, 1, 7)]
    arrive(r_dm)
    dcs[...] = dot_nt(rdm[...].reshape(256, 1152), wm[...].reshape(256, 1152)).astype(BF16)
    r_dc = [send(dcs, dcr.at[e - 1], tdev(e)) for e in range(1, 4)]
    arrive(r_dc)
    d_cond = dcs[...].astype(F32)
    for e in range(3):
        d_cond = d_cond + dcr[e].astype(F32)
    d_cond = d_cond.astype(BF16)
    dcz[...] = d_cond.reshape(8, rows, 256)
    r_dz = [send(dcz.at[d], dch.at[z], zdev(-d)) for d in range(1, 8)]
    dch[z] = dcz[0]

    arrive(r_pk)
    turned = d_cond.astype(F32).T.astype(BF16)
    for i in range(4):
        cols = pl.ds(512 * i, 512)
        cg = dot_nn(turned, pkg[:, :, cols].reshape(256, 512))
        cgs[:, :, cols] = cg.astype(BF16).reshape(8, 32, 512)
    r_cg = []
    for d in range(1, 8):
        dev = pdev(d)
        r_cg.append(send(cgs.at[dev[0]], rcg.at[d - 1], dev))

    arrive(r_dz)
    back = jnp.concatenate([dch[zz].astype(F32) for zz in range(8)], axis=1).T
    pieces = []
    for pp in range(8):
        for zz in range(8):
            pieces.append(back[256 * zz + 32 * pp : 256 * zz + 32 * pp + 24])
    back = jnp.concatenate(pieces, axis=0).T.astype(BF16)
    for i in range(4):
        cols = pl.ds(512 * i, 512)
        row_o[:, :, cols] = dot_nn(back, wc[:, cols]).reshape(4, 8, 512).astype(BF16)

    arrive(r_cg)
    for i in range(4):
        cols = pl.ds(512 * i, 512)
        cg = cgs[p, :, cols].astype(F32)
        for e in range(7):
            cg = cg + rcg[e, :, cols].astype(F32)
        conn_o[:, cols] = cg[:24] * (1.0 / 64.0)
    for c in sent:
        c.wait_send()


def local(hidden, positions, image_tokens, groups, latents, out_grad, w_conn, w_mod, w_up, w_down):
    w_mod2 = jnp.pad(w_mod.reshape(24, 1152), ((0, 8), (0, 0)))
    vm = pl.BlockSpec(memory_space=pltpu.VMEM)
    sm = pl.BlockSpec(memory_space=pltpu.SMEM)
    hb = pl.BlockSpec(memory_space=pl.ANY)
    V = pltpu.VMEM
    n_copies = 7 * 14 + 7 + 3 * 2 + 7
    return pl.pallas_call(
        kernel,
        out_shape=(
            jax.ShapeDtypeStruct((4, 8, 384), BF16),
            jax.ShapeDtypeStruct((4, 8, 2048), BF16),
            jax.ShapeDtypeStruct((24, 2048), F32),
        ),
        in_specs=[sm, sm, sm, hb, vm, vm, hb, vm, hb, hb],
        out_specs=(vm, vm, vm),
        scratch_shapes=[
            V((4, 128, 2048), BF16),
            V((1536, 2048), BF16),
            V((1536, 768), BF16),
            V((1536, 768), BF16),
            V((8, 32, 1152), BF16),
            V((32, 2048), BF16),
            V((8, 32, 2048), BF16),
            V((32, 1536), BF16),
            V((3, 32, 1536), BF16),
            V((8, 32, 256), BF16),
            V((8, 32, 256), BF16),
            V((8, 32, 1152), BF16),
            V((8, 32, 1152), BF16),
            V((8, 16, 768), BF16),
            V((8, 128, 768), BF16),
            V((256, 768), F32),
            V((8, 128, 384), BF16),
            V((7, 128, 384), BF16),
            V((8, 128, 384), BF16),
            V((7, 128, 384), BF16),
            V((8, 16, 768), BF16),
            V((8, 16, 768), BF16),
            V((8, 32, 1152), BF16),
            V((256, 256), BF16),
            V((3, 256, 256), BF16),
            V((8, 32, 256), BF16),
            V((8, 32, 256), BF16),
            V((8, 32, 2048), BF16),
            V((7, 32, 2048), BF16),
            pltpu.SemaphoreType.DMA((8,)),
            pltpu.SemaphoreType.DMA((n_copies,)),
            pltpu.SemaphoreType.DMA((n_copies,)),
        ],
        compiler_params=pltpu.CompilerParams(
            collective_id=0, has_side_effects=True, vmem_limit_bytes=56 * 2**20
        ),
        cost_estimate=pl.CostEstimate(
            flops=6_000_000_000, bytes_accessed=16_000_000, transcendentals=200_000
        ),
    )(groups, image_tokens, positions, hidden, latents, out_grad, w_conn, w_mod2, w_up, w_down)


def solution(mesh):
    placed = (
        P(("pp", "dp"), None, "tp"),
        P(("pp", "dp"), None),
        P(("pp", "dp")),
        P(("pp", "dp"), None),
        P(("pp", "dp"), None, None),
        P(("pp", "dp"), None, "tp"),
        P(None, "tp"),
        P(("pp", "dp"), None, "tp"),
        P("dp", "pp", "tp"),
        P("dp", "pp", "tp"),
    )
    return jax.shard_map(
        local,
        mesh=mesh,
        in_specs=placed,
        out_specs=(P(("pp", "dp"), None, "tp"), P(("pp", "dp"), None, "tp"), P(("pp", "dp"), "tp")),
        check_vma=False,
    )
```

time: 1260 us -> 191 us (0.15)
  waiting for transfers between devices: 1100 us -> 0 us
  Pallas kernels: 0 us -> 181 us
  blocking collectives: 57.2 us -> 0 us
  matrix products: 42.4 us -> 0 us
  starting transfers between devices: 18 us -> 0 us
  between operations: 15.7 us -> 0.64 us
    reduce_scatter x1 -> x0, waiting for transfers between devices: 789 us -> none  [local(): lax.psum_scatter(jnp.einsum('rc,rd->cd', d_cond, got_rows, preferred_elem...]
    all_gather x3 -> x0, waiting for transfers between devices: 205 us -> none  [the longest x1 77.9 us: local(): lax.all_gather(w_down, 'pp', axis=1, tiled=True)]
    pallas_call x0 -> x1, Pallas kernels: none -> 181 us  [local(): pl.pallas_call(kernel, out_shape=(jax.ShapeDtypeStruct((4, 8, 384), BF16)...]
    psum x2 -> x0, waiting for transfers between devices: 42.6 us -> none  [the longest x1 42.6 us: local(): lax.psum(d_cond_part.astype(jnp.bfloat16), 'tp').astype(jnp.float32)]
    dot_general x14 -> x0, matrix products: 42.4 us -> none  [the longest x1 7.42 us: local(): jnp.einsum('rc,rd->cd', d_cond, got_rows, preferred_element_type=jnp.floa...]
    all_to_all x2 -> x0, blocking collectives: 38.2 us -> none  [the longest x1 25.1 us: local(): lax.all_to_all(in_groups(picked), 'dp', split_axis=0, concat_axis=0, tile...]
    all_to_all x4 -> x0, waiting for transfers between devices: 33.2 us -> none  [the longest x1 19.4 us: local(): lax.all_to_all(grad_rows.reshape(group_total, CAP, image_len, row_depth),...]
    unnamed x10 -> x0, waiting for transfers between devices: 25.2 us -> none
  transfers between devices with their start and end apart: 12 -> 0, of which waited for: 10 -> 0; matrix products, arithmetic and copies ran while one was open for 3% -> 0% of each run, Pallas kernels for 0% -> 0%
where the time goes in v1:
time: 191 us; the launch traced here: 189 us
  Pallas kernels  181 us (95%)
  local copies, waits for them, and re-layouts  7.3 us (4%)
    pallas_call x1, Pallas kernels, local(): pl.pallas_call(kernel, out_shape=(jax.ShapeDtypeStruct((4, 8, 384), BF16)...  181 us
    unnamed x4, local copies, waits for them, and re-layouts  5.84 us

profile of v1, /device:TPU:1, one launch (start us, length us, event | category | flops | bytes accessed | tf_op | source)
XLA Modules:
  0.0 189.4 jit_solution(6993595651244814247)
XLA Ops:
  0.6 1.3 copy.16.groups
  1.9 0.8 copy.17
  2.8 0.6 pad.4.w_mod
  3.4 181.4 %shard_map.121 = (bf16[4,8,384]{2,1,0:T(8,128)(2,1)}, bf16[4,8,2048]{2,1,0:T(8,128)(2,1)}, f32[24,2048]{1,0:T(8,128)}) custom-call(s32[4,1]{1,0:T(4,128)} %copy.16.groups, s32[4]{0:T(128)} %tokens.1, s32[4,8]{1,0:T(4,128)} %positions.1, bf16[4,128,2048]{2,1,0:T(8,128)(2,1)} %hidden.1, bf16[4,8,1536]{2,1,0:T(8,128)(2,1)} %latents.1, ...), custom_call_target="tpu_custom_call" | custom-call | flops 6000000000 | bytes 16000000 | tf_op jit(solution)/shard_map/pallas_call | solution.py:330
  184.8 1.3 copy.21
  186.2 1.6 copy.22
  187.8 1.6 copy.23

commit v2 on v1

v2 whole, which is shorter than its diff:
```python
import functools

import jax
import jax.numpy as jnp
from jax import lax
from jax.experimental import pallas as pl
from jax.experimental.pallas import tpu as pltpu
from jax.sharding import PartitionSpec as P

MESH = pl.DeviceIdType.MESH
CAP = 2
F32 = jnp.float32
BF16 = jnp.bfloat16
tanh_coef = 0.7978845608028654
cubic_term = 0.044715


def gelu_pair(preact):
    inner_arg = tanh_coef * (preact + cubic_term * preact * preact * preact)
    tanh_value = jnp.tanh(inner_arg)
    gelu_value = 0.5 * preact * (1.0 + tanh_value)
    gelu_slope = 0.5 * (1.0 + tanh_value) + 0.5 * preact * (
        1.0 - tanh_value * tanh_value
    ) * tanh_coef * (1.0 + 3.0 * cubic_term * preact * preact)
    return (gelu_value, gelu_slope)


def dot_nn(a, b):
    return lax.dot_general(a, b, (((1,), (0,)), ((), ())), preferred_element_type=F32)


def dot_nt(a, b):
    return lax.dot_general(a, b, (((1,), (1,)), ((), ())), preferred_element_type=F32)


def kernel(
    groups, tokens, positions, hidden, latents_h, out_grad_h, w_conn, w_mod_h, w_up, w_down,
    gen_o, row_o, conn_o,
    hid, latents, out_grad, w_mod, wc, wu, wd, wmx, wm, pick, pkg,
    cpb, cpr, cst, cz, mps, mrs,
    slot, hd, slope_s, ffs, fsib, fsum, rff, dhs, dsib, dsum, rdh, rets, ret,
    rdm, dcs, dcr, dcz, dcx, dcf, dch, cgs, rcg,
    lsem, ssem, rsem, jsem,
):
    p, z, t = lax.axis_index("pp"), lax.axis_index("dp"), lax.axis_index("tp")
    yh, x = p // 4, lax.rem(p, 4)
    pair, par = z // 2, lax.rem(z, 2)
    core = lax.rem(t, 2)
    ypos = yh * 2 + t // 2
    m = yh * 4 + t
    rows = 32

    def zdev(d):
        return (p, lax.rem(z + d + 8, 8), t)

    def pdev(d):
        return (lax.rem(p + d, 8), z, t)

    def xdev(d):
        return (yh * 4 + lax.rem(x + d, 4), z, t)

    def tdev(e):
        return (p, z, lax.rem(t + e, 4))

    def yplace(d):
        return lax.rem(ypos + d, 4)

    def ydev(d):
        yy = yplace(d)
        return ((yy // 2) * 4 + x, z, lax.rem(yy, 2) * 2 + core)

    twin = (p, z, t + 1 - 2 * core)
    partner = (p, z + 1 - 2 * par, t)

    barrier = pltpu.get_barrier_semaphore()
    peers = [zdev(d) for d in range(1, 8)]
    peers += [pdev(d) for d in range(1, 8)]
    peers += [tdev(e) for e in range(1, 4)]
    peers += [ydev(d) for d in (1, 3)]
    for dev in peers:
        pl.semaphore_signal(barrier, inc=1, device_id=dev, device_id_type=MESH)
    owner = pair == t
    for j in range(4):

        @pl.when(jnp.logical_not(jnp.logical_and(owner, pair == j)))
        def _():
            pl.semaphore_signal(
                barrier, inc=1, device_id=(p, 2 * j + par, pair), device_id_type=MESH
            )

    loc = []

    def load(src, dst):
        c = pltpu.make_async_copy(src, dst, lsem.at[len(loc)])
        c.start()
        loc.append(c)
        return c

    c_hid = load(hidden, hid)
    c_wm = load(w_mod_h, w_mod)
    c_wc = [
        load(w_conn.at[pl.ds(512 * i, 512)], wc.at[pl.ds(512 * i, 512)]) for i in range(3)
    ]
    c_lat = load(latents_h, latents)
    c_og = load(out_grad_h, out_grad)

    seq_iota = lax.broadcasted_iota(jnp.int32, (8, 128), 1)
    row_iota = lax.broadcasted_iota(jnp.int32, (8, 128), 0)
    c_hid.wait()
    parts = []
    for s in range(4):
        at = jnp.zeros((8, 128), jnp.int32)
        for i in range(8):
            at = jnp.where(row_iota == i, positions[s, i], at)
        sel = jnp.where(seq_iota == at, 1.0, 0.0).astype(BF16)
        parts.append(dot_nn(sel, hid[s]))
    pick[...] = jnp.concatenate(parts, axis=0).astype(BF16)
    pkg[par * 4 + pair] = pick[...]

    parts = []
    for i in range(3):
        c_wc[i].wait()
        parts.append(dot_nt(pick[...], wc[pl.ds(512 * i, 512), :]))
    cond = jnp.concatenate(parts, axis=1).T
    pieces = []
    for k in range(4):
        for pp in range(8):
            pieces.append(cond[192 * pp + 48 * k : 192 * pp + 48 * k + 48])
    cond = jnp.concatenate(pieces, axis=0).T.astype(BF16)
    for k in range(4):
        cpb[k] = cond[:, 384 * k : 384 * k + 384]
    c_wm.wait()
    for k in range(3):
        wmx[par, 0:24, 384 * k : 384 * k + 384] = w_mod[k]
    wmx[par, 24:32, :] = jnp.zeros((8, 1152), BF16)
    pl.semaphore_wait(barrier, len(peers) + 4 - jnp.where(owner, 1, 0))

    sent = []

    def send(src, dst, dev):
        k = len(sent)
        c = pltpu.make_async_remote_copy(
            src_ref=src, dst_ref=dst, send_sem=ssem.at[k], recv_sem=rsem.at[k],
            device_id=dev, device_id_type=MESH,
        )
        c.start()
        sent.append(c)
        return c

    def arrive(copies):
        for c in copies:
            c.wait_recv()

    x_wm = send(wmx.at[par], wmx.at[par], partner)
    r_cp = []
    for e in (2, 3, 1):
        r_cp.append(send(cpb.at[lax.rem(t + e, 4)], cpr.at[e - 1], tdev(e)))

    def half(ref, which):
        return ref.at[0, :, pl.ds(pl.multiple_of(768 * which, 768), 768)]

    def block(buf, who, xx, lo=0, n=192):
        return buf.at[pl.ds(pl.multiple_of(192 * (who * 4 + xx) + lo, 32), n)]

    xm, xp = lax.rem(x + 3, 4), lax.rem(x + 1, 4)

    def to_neighbours(src, dst):
        return [send(src, dst, xdev(1)), send(src, dst, xdev(3))]

    def hand_over(buf, who, near):
        arrive(near[:1])
        top = block(buf, who, xm, 0, 96)
        c1 = send(top, top, xdev(1))
        arrive(near[1:])
        low = block(buf, who, xp, 96, 96)
        return [c1, send(low, low, xdev(3))]

    own_u, own_d = block(wu, yh, x), block(wd, yh, x)
    oth_u, oth_d = block(wu, 1 - yh, x), block(wd, 1 - yh, x)
    y_wu = send(half(w_up, 1 - yh), own_u, pdev(4))
    au = to_neighbours(half(w_up, yh), own_u)
    c_wu = load(half(w_up, yh), own_u)
    c_wd = load(half(w_down, yh), own_d)
    r_pk = [send(pick, pkg.at[par * 4 + pair], zdev(d)) for d in (1, 7)]
    arrive([x_wm])
    wm[p] = jnp.concatenate(
        [wmx[0].astype(F32)[:24], wmx[1].astype(F32)[:24]], axis=0
    ).astype(BF16)
    r_wm = [send(wm.at[p], wm.at[p], pdev(d)) for d in (4, 2, 6, 1, 7, 3, 5)]

    c_lat.wait()
    c_og.wait()
    lat = latents[...].astype(F32).reshape(rows, 1536)
    mean = jnp.mean(lat, axis=-1, keepdims=True)
    cent = lat - mean
    var = jnp.mean(cent * cent, axis=-1, keepdims=True)
    inv = 1.0 / jnp.sqrt(var + 1e-06)
    mine = pl.ds(pl.multiple_of(t * 384, 384), 384)
    lat_t = latents[:, :, mine].astype(F32).reshape(rows, 384)
    normed = (lat_t - mean) * inv
    cot = out_grad[...].astype(F32).reshape(rows, 384)

    gs = [groups[s] for s in range(4)]
    places = []
    for s in range(4):
        rank = 0
        for q in range(s):
            rank = rank + jnp.where(gs[q] == gs[s], 1, 0)
        places.append(gs[s] * CAP + rank)
    big_r = lax.broadcasted_iota(jnp.int32, (128, rows), 0)
    big_c = lax.broadcasted_iota(jnp.int32, (128, rows), 1)
    place = jnp.zeros((128, rows), jnp.int32)
    for s in range(4):
        place = jnp.where(big_c // 8 == s, places[s], place)
    onehot = jnp.where(big_r == place * 8 + lax.rem(big_c, 8), 1.0, 0.0).astype(BF16)
    flip_r = lax.broadcasted_iota(jnp.int32, (rows, 128), 0)
    flip_c = lax.broadcasted_iota(jnp.int32, (rows, 128), 1)
    place_f = jnp.zeros((rows, 128), jnp.int32)
    for s in range(4):
        place_f = jnp.where(flip_r // 8 == s, places[s], place_f)
    onehot_f = jnp.where(flip_c == place_f * 8 + lax.rem(flip_r, 8), 1.0, 0.0).astype(BF16)
    one_r = lax.broadcasted_iota(jnp.int32, (rows, 384), 0)
    used = jnp.zeros((rows, 384), jnp.int32)
    for s in range(4):
        used = jnp.where(one_r // 8 == s, tokens[s], used)
    valid = jnp.where(lax.rem(one_r, 8) < used, 1.0, 0.0)

    arrive(r_cp)
    cond = cpb[t].astype(F32)
    for e in range(3):
        cond = cond + cpr[e].astype(F32)
    cst[...] = cond.astype(BF16)

    def cond_copy(e):
        return pltpu.make_async_remote_copy(
            src_ref=cst, dst_ref=cz.at[pair], send_sem=jsem.at[e], recv_sem=jsem.at[4 + pair],
            device_id=(p, 2 * t + par, lax.rem(t + e, 4)), device_id_type=MESH,
        )

    here = pltpu.make_async_copy(cst, cz.at[pair], jsem.at[4 + pair])
    for e in (2, 1, 3):
        cond_copy(e).start()

    @pl.when(owner)
    def _():
        here.start()

    @pl.when(jnp.logical_not(owner))
    def _():
        cond_copy(0).start()

    y_wd = send(half(w_down, 1 - yh), own_d, pdev(4))
    du = hand_over(wu, yh, au)
    arrive(r_wm)
    for j in range(4):
        pltpu.make_async_copy(cst, cz.at[j], jsem.at[4 + j]).wait()

    wmod = wm[...].reshape(384, 1152)
    pooled = cz[...].reshape(128, 384)
    mps[...] = dot_nn(pooled, wmod).astype(BF16).reshape(4, rows, 1152)
    r_mr = []
    for d in (2, 1, 3):
        dev = zdev(2 * d)
        r_mr.append(send(mps.at[dev[1] // 2], mrs.at[d - 1], dev))
    mod = mps[pair].astype(F32)
    arrive([y_wu])
    cu = to_neighbours(oth_u, oth_u)
    ad = to_neighbours(half(w_down, yh), own_d)
    arrive(r_mr)
    for d in range(3):
        mod = mod + mrs[d].astype(F32)
    shift, scale, gate = mod[:, :384], mod[:, 384:768], mod[:, 768:]

    h_in = (normed * (1.0 + scale) + shift).astype(BF16)
    d_out = (gate * cot).astype(BF16)
    packed = dot_nn(onehot, jnp.concatenate([h_in, d_out], axis=1)).astype(BF16)
    slot[...] = packed.reshape(8, 16, 768)
    r_sl = []
    for d in (4, 3, 5, 2, 6, 1, 7):
        dev = zdev(d)
        r_sl.append(send(slot.at[dev[1]], hd.at[m, pl.ds(16 * d, 16)], dev))
    hd[m, pl.ds(0, 16)] = slot[z]
    arrive(r_sl)

    def piece(k, lo):
        return hd.at[k, :, pl.ds(lo, 384)]

    first = []
    for lo in (0, 384):
        first.append([send(piece(m, lo), piece(m, lo), ydev(d)) for d in (2, 1, 3)])
    eu = hand_over(wu, 1 - yh, cu)
    arrive([y_wd])
    cd = to_neighbours(oth_d, oth_d)
    dd = hand_over(wd, yh, ad)
    second = [[send(piece(m, lo), piece(m, lo), twin)] for lo in (0, 384)]
    r_pk += [send(pick, pkg.at[par * 4 + pair], zdev(d)) for d in (4, 3, 5, 2, 6)]

    def hand_on(which, lo):
        for c, d in zip(first[which], (2, 1, 3)):
            arrive([c])
            k = 2 * lax.rem(ypos + 4 - d, 4) + core
            second[which].append(send(piece(k, lo), piece(k, lo), twin))

    hand_on(0, 0)
    arrive(second[0])
    c_wu.wait()
    arrive(du + eu)

    def both(k, lo):
        return jnp.concatenate([hd[k, :, lo : lo + 384], hd[4 + k, :, lo : lo + 384]], axis=0)

    def reduce_out(val, weight, out, sib, whole, got):
        for k in range(4):
            res = dot_nt(val, weight[384 * k : 384 * k + 384, :]).astype(BF16)
            out[k % 2, k // 2] = res[:128]
            out[k % 2, 2 + k // 2] = res[128:]
        return [send(out.at[1 - core, d], sib.at[d], twin) for d in range(4)]

    def reduce_chips(ex, out, sib, whole, got):
        arrive(ex)
        for d in range(4):
            whole[d] = (out[core, d].astype(F32) + sib[d].astype(F32)).astype(BF16)
        return [send(whole.at[yplace(d)], got.at[d - 1], ydev(d)) for d in (2, 1, 3)]

    def reduce_end(ex, whole, got):
        arrive(ex)
        res = whole[ypos].astype(F32)
        for d in range(3):
            res = res + got[d].astype(F32)
        return res.astype(BF16).reshape(8, 16, 384)

    pre = dot_nn(both(0, 0), wu[0:384, :])
    for k in range(1, 4):
        pre = pre + dot_nn(both(k, 0), wu[384 * k : 384 * k + 384, :])
    value, slope = gelu_pair(pre)
    act = value.astype(BF16)
    slope_s[...] = slope
    hand_on(1, 384)
    c_wd.wait()
    ed = hand_over(wd, 1 - yh, cd)
    arrive(dd + ed)
    ff_ex = reduce_out(act, wd, ffs, fsib, fsum, rff)
    arrive(second[1])
    d_act = dot_nn(both(0, 384), wd[0:384, :])
    for k in range(1, 4):
        d_act = d_act + dot_nn(both(k, 384), wd[384 * k : 384 * k + 384, :])
    d_pre = (d_act * slope_s[...]).astype(BF16)
    r_ff = reduce_chips(ff_ex, ffs, fsib, fsum, rff)
    dh_ex = reduce_out(d_pre, wu, dhs, dsib, dsum, rdh)
    r_dh = reduce_chips(dh_ex, dhs, dsib, dsum, rdh)
    rets[:, :, pl.ds(0, 384)] = reduce_end(r_ff, fsum, rff)
    rets[:, :, pl.ds(384, 384)] = reduce_end(r_dh, dsum, rdh)
    r_rt = [send(rets.at[d], ret.at[z], zdev(-d)) for d in (4, 3, 5, 2, 6, 1, 7)]
    ret[z] = rets[0]
    arrive(r_rt)
    home = dot_nn(onehot_f, ret[...].reshape(128, 768))
    ff_out, d_hin = home[:, :384], home[:, 384:]
    d_mod = jnp.concatenate(
        [valid * d_hin, valid * (d_hin * normed), valid * (cot * ff_out)], axis=1
    )
    rdm[pair] = d_mod.astype(BF16)
    r_dm = [send(rdm.at[pair], rdm.at[pair], zdev(2 * d)) for d in (2, 1, 3)]
    gen_o[...] = (valid * (lat_t + gate * ff_out)).reshape(4, 8, 384).astype(BF16)
    arrive(r_dm)
    dcs[...] = dot_nt(rdm[...].reshape(128, 1152), wm[...].reshape(384, 1152)).astype(BF16)
    r_dc = [send(dcs, dcr.at[e - 1], tdev(e)) for e in (2, 3, 1)]
    arrive(r_dc)
    d_cond = dcs[...].astype(F32)
    for e in range(3):
        d_cond = d_cond + dcr[e].astype(F32)
    d_cond = d_cond.astype(BF16)
    turned = d_cond.astype(F32).T
    for h in range(2):
        dcx[h] = jnp.concatenate(
            [turned[48 * pp + 24 * h : 48 * pp + 24 * h + 24] for pp in range(8)], axis=0
        ).astype(BF16)
    r_df = [send(dcx.at[1 - par], dcf.at[par], partner)]
    dcz[...] = d_cond.reshape(4, rows, 384)
    r_dz = []
    for d in (2, 1, 3):
        dev = zdev(2 * d)
        r_dz.append(send(dcz.at[dev[1] // 2], dch.at[pair], dev))
    dch[pair] = dcz[pair]
    dcf[par] = dcx[par]

    arrive(r_pk)
    arrive(r_df)
    r_cg = []
    for h in range(2):
        sides = []
        for i in range(2):
            cols = pl.ds(1024 * h + 512 * i, 512)
            res = dot_nn(dcf[0], pkg[0:4, :, cols].reshape(128, 512))
            res = res + dot_nn(dcf[1], pkg[4:8, :, cols].reshape(128, 512))
            sides.append(res.reshape(8, 24, 512))
        cgs[h] = jnp.concatenate(
            [sides[0][:, :16], sides[1][:, :16], sides[0][:, 16:24], sides[1][:, 16:24]], axis=1
        ).astype(BF16)
        for d in (4, 2, 6, 1, 7, 3, 5):
            dev = pdev(d)
            r_cg.append(send(cgs.at[h, dev[0]], rcg.at[h, d - 1], dev))

    arrive(r_dz)
    back = jnp.concatenate([dch[q].astype(F32) for q in range(4)], axis=1).T
    pieces = []
    for pp in range(8):
        for q in range(4):
            pieces.append(back[384 * q + 48 * pp : 384 * q + 48 * pp + 48])
    back = jnp.concatenate(pieces, axis=0).T.astype(BF16)
    for i in range(4):
        cols = pl.ds(512 * i, 512)
        row_o[:, :, cols] = dot_nn(back, wc[:, cols]).reshape(4, 8, 512).astype(BF16)

    for h in range(2):
        arrive(r_cg[7 * h : 7 * h + 7])
        cg = cgs[h, p].astype(F32)
        for e in range(7):
            cg = cg + rcg[h, e].astype(F32)
        cg = cg * (1.0 / 64.0)
        for i in range(2):
            cols = pl.ds(1024 * h + 512 * i, 512)
            conn_o[0:16, cols] = cg[16 * i : 16 * i + 16]
            conn_o[16:24, cols] = cg[32 + 8 * i : 40 + 8 * i]
    for c in sent:
        c.wait_send()
    for e in range(1, 4):
        cond_copy(e).wait_send()

    @pl.when(jnp.logical_not(owner))
    def _():
        cond_copy(0).wait_send()


def hand_out(gen, row, conn, gen_o, row_o, conn_o):
    gen_o[...] = gen[...]
    row_o[...] = row[...]
    conn_o[...] = conn[...]


def local(hidden, positions, image_tokens, groups, latents, out_grad, w_conn, w_mod, w_up, w_down):
    vm = pl.BlockSpec(memory_space=pltpu.VMEM)
    sm = pl.BlockSpec(memory_space=pltpu.SMEM)
    hb = pl.BlockSpec(memory_space=pl.ANY)
    V = pltpu.VMEM
    n_copies = 144
    outs = pl.pallas_call(
        kernel,
        out_shape=(
            jax.ShapeDtypeStruct((4, 8, 384), BF16),
            jax.ShapeDtypeStruct((4, 8, 2048), BF16),
            jax.ShapeDtypeStruct((24, 2048), F32),
        ),
        in_specs=[sm, sm, sm, hb, hb, hb, hb, hb, hb, hb],
        out_specs=(vm, vm, vm),
        scratch_shapes=[
            V((4, 128, 2048), BF16),
            V((4, 8, 1536), BF16),
            V((4, 8, 384), BF16),
            V((3, 24, 384), BF16),
            V((1536, 2048), BF16),
            V((1536, 768), BF16),
            V((1536, 768), BF16),
            V((2, 32, 1152), BF16),
            V((8, 48, 1152), BF16),
            V((32, 2048), BF16),
            V((8, 32, 2048), BF16),
            V((4, 32, 384), BF16),
            V((3, 32, 384), BF16),
            V((32, 384), BF16),
            V((4, 32, 384), BF16),
            V((4, 32, 1152), BF16),
            V((3, 32, 1152), BF16),
            V((8, 16, 768), BF16),
            V((8, 128, 768), BF16),
            V((256, 768), F32),
            V((2, 4, 128, 384), BF16),
            V((4, 128, 384), BF16),
            V((4, 128, 384), BF16),
            V((3, 128, 384), BF16),
            V((2, 4, 128, 384), BF16),
            V((4, 128, 384), BF16),
            V((4, 128, 384), BF16),
            V((3, 128, 384), BF16),
            V((8, 16, 768), BF16),
            V((8, 16, 768), BF16),
            V((4, 32, 1152), BF16),
            V((128, 384), BF16),
            V((3, 128, 384), BF16),
            V((4, 32, 384), BF16),
            V((2, 192, 128), BF16),
            V((2, 192, 128), BF16),
            V((4, 32, 384), BF16),
            V((2, 8, 48, 512), BF16),
            V((2, 7, 48, 512), BF16),
            pltpu.SemaphoreType.DMA((12,)),
            pltpu.SemaphoreType.DMA((n_copies,)),
            pltpu.SemaphoreType.DMA((n_copies,)),
            pltpu.SemaphoreType.DMA((8,)),
        ],
        compiler_params=pltpu.CompilerParams(
            collective_id=0, has_side_effects=True, vmem_limit_bytes=56 * 2**20
        ),
        cost_estimate=pl.CostEstimate(
            flops=6_000_000_000, bytes_accessed=16_000_000, transcendentals=200_000
        ),
    )(
        groups.reshape(4), image_tokens, positions, hidden, latents, out_grad, w_conn,
        jnp.transpose(w_mod, (1, 0, 2)), w_up, w_down,
    )
    return pl.pallas_call(
        hand_out,
        out_shape=tuple(jax.ShapeDtypeStruct(o.shape, o.dtype) for o in outs),
        in_specs=[vm, vm, vm],
        out_specs=(vm, vm, vm),
    )(*outs)


def solution(mesh):
    placed = (
        P(("pp", "dp"), None, "tp"),
        P(("pp", "dp"), None),
        P(("pp", "dp")),
        P(("pp", "dp"), None),
        P(("pp", "dp"), None, None),
        P(("pp", "dp"), None, "tp"),
        P(None, "tp"),
        P(("pp", "dp"), None, "tp"),
        P("dp", "pp", "tp"),
        P("dp", "pp", "tp"),
    )
    return jax.shard_map(
        local,
        mesh=mesh,
        in_specs=placed,
        out_specs=(P(("pp", "dp"), None, "tp"), P(("pp", "dp"), None, "tp"), P(("pp", "dp"), "tp")),
        check_vma=False,
    )
```

time: 191 us -> 125 us (0.65)
  Pallas kernels: 181 us -> 125 us
  local copies, waits for them, and re-layouts: 7.3 us -> 0 us
    pallas_call x1, Pallas kernels: 181 us -> 123 us  [local(): pl.pallas_call(kernel, out_shape=(jax.ShapeDtypeStruct((4, 8, 384), BF16)...]
    unnamed x4 -> x0, local copies, waits for them, and re-layouts: 5.84 us -> none
where the time goes in v2:
time: 125 us
  Pallas kernels  125 us (100%)
    pallas_call x1, Pallas kernels, local(): pl.pallas_call(kernel, out_shape=(jax.ShapeDtypeStruct((4, 8, 384), BF16)...  123 us

profile of v2, /device:TPU:1, one launch (start us, length us, event | category | flops | bytes accessed | tf_op | source)
XLA Modules:
  0.0 125.2 jit_solution(15407930099951134624)
XLA Ops:
  0.6 122.8 %shard_map.121 = (bf16[4,8,384]{2,1,0:T(8,128)(2,1)}, bf16[4,8,2048]{2,1,0:T(8,128)(2,1)}, f32[24,2048]{1,0:T(8,128)}) custom-call(s32[4]{0:T(128)} %bitcast.3, s32[4]{0:T(128)} %tokens.1, s32[4,8]{1,0:T(4,128)} %positions.1, bf16[4,128,2048]{2,1,0:T(8,128)(2,1)} %hidden.1, bf16[4,8,1536]{2,1,0:T(8,128)(2,1)} %latents_h.1, bf16[4,8,384]{2,1,0:T(8,128)(2,1)} %out_grad_h.1, ...), custom_call_target="tpu_custom_call" | custom-call | flops 6000000000 | bytes 16000000 | tf_op jit(solution)/shard_map/pallas_call | solution.py:446
  123.4 1.7 %shard_map.122 = (bf16[4,8,384]{2,1,0:T(8,128)(2,1)}, bf16[4,8,2048]{2,1,0:T(8,128)(2,1)}, f32[24,2048]{1,0:T(8,128)}) custom-call(bf16[4,8,384]{2,1,0:T(8,128)(2,1)} %get-tuple-element.6.gen, bf16[4,8,2048]{2,1,0:T(8,128)(2,1)} %get-tuple-element.7.row, f32[24,2048]{1,0:T(8,128)} %get-tuple-element.8.conn), custom_call_target="tpu_custom_call" | custom-call | tf_op jit(solution)/shard_map/pallas_call | solution.py:510

commit v3 on v2

--- a/solution.py
+++ b/solution.py
@@ -37,9 +37,9 @@
     groups, tokens, positions, hidden, latents_h, out_grad_h, w_conn, w_mod_h, w_up, w_down,
     gen_o, row_o, conn_o,
     hid, latents, out_grad, w_mod, wc, wu, wd, wmx, wm, pick, pkg,
-    cpb, cpr, cst, cz, mps, mrs,
+    cpb, cpr, cst, cz, mps, mrs, mpg, mrg,
     slot, hd, slope_s, ffs, fsib, fsum, rff, dhs, dsib, dsum, rdh, rets, ret,
-    rdm, dcs, dcr, dcz, dcx, dcf, dch, cgs, rcg,
+    rdm, rdm2, dcs, dcr, dcz, dcx, dcf, dch, cgs, rcg,
     lsem, ssem, rsem, jsem,
 ):
     p, z, t = lax.axis_index("pp"), lax.axis_index("dp"), lax.axis_index("tp")
@@ -75,6 +75,7 @@
     barrier = pltpu.get_barrier_semaphore()
     peers = [zdev(d) for d in range(1, 8)]
     peers += [pdev(d) for d in range(1, 8)]
+    peers += [(lax.rem(p + d, 8), partner[1], t) for d in range(1, 8)]
     peers += [tdev(e) for e in range(1, 4)]
     peers += [ydev(d) for d in (1, 3)]
     for dev in peers:
@@ -131,8 +132,7 @@
         cpb[k] = cond[:, 384 * k : 384 * k + 384]
     c_wm.wait()
     for k in range(3):
-        wmx[par, 0:24, 384 * k : 384 * k + 384] = w_mod[k]
-    wmx[par, 24:32, :] = jnp.zeros((8, 1152), BF16)
+        wmx[par, p, :, 384 * k : 384 * k + 384] = w_mod[k]
     pl.semaphore_wait(barrier, len(peers) + 4 - jnp.where(owner, 1, 0))
 
     sent = []
@@ -151,10 +151,16 @@
         for c in copies:
             c.wait_recv()
 
-    x_wm = send(wmx.at[par], wmx.at[par], partner)
+    far = (4, 2, 6, 1, 7, 3, 5)
     r_cp = []
     for e in (2, 3, 1):
         r_cp.append(send(cpb.at[lax.rem(t + e, 4)], cpr.at[e - 1], tdev(e)))
+    r_wm = [send(wmx.at[par, p], wmx.at[par, p], pdev(d)) for d in far]
+    x_wm = [send(wmx.at[par, p], wmx.at[par, p], partner)]
+    for d in far:
+        x_wm.append(
+            send(wmx.at[par, p], wmx.at[par, p], (lax.rem(p + d, 8), partner[1], t))
+        )
 
     def half(ref, which):
         return ref.at[0, :, pl.ds(pl.multiple_of(768 * which, 768), 768)]
@@ -177,16 +183,9 @@
 
     own_u, own_d = block(wu, yh, x), block(wd, yh, x)
     oth_u, oth_d = block(wu, 1 - yh, x), block(wd, 1 - yh, x)
-    y_wu = send(half(w_up, 1 - yh), own_u, pdev(4))
-    au = to_neighbours(half(w_up, yh), own_u)
     c_wu = load(half(w_up, yh), own_u)
     c_wd = load(half(w_down, yh), own_d)
     r_pk = [send(pick, pkg.at[par * 4 + pair], zdev(d)) for d in (1, 7)]
-    arrive([x_wm])
-    wm[p] = jnp.concatenate(
-        [wmx[0].astype(F32)[:24], wmx[1].astype(F32)[:24]], axis=0
-    ).astype(BF16)
-    r_wm = [send(wm.at[p], wm.at[p], pdev(d)) for d in (4, 2, 6, 1, 7, 3, 5)]
 
     c_lat.wait()
     c_og.wait()
@@ -249,65 +248,82 @@
     def _():
         cond_copy(0).start()
 
-    y_wd = send(half(w_down, 1 - yh), own_d, pdev(4))
+    y_wu = send(half(w_up, 1 - yh), own_u, pdev(4))
+    au = to_neighbours(half(w_up, yh), own_u)
+    for c, d in zip(x_wm, (0,) + far):
+        arrive([c])
+        if d > 0:
+            arrive([r_wm[far.index(d)]])
+        pd = lax.rem(p + 8 - d, 8)
+        wm[pd] = jnp.concatenate(
+            [wmx[0, pd].astype(F32), wmx[1, pd].astype(F32)], axis=0
+        ).astype(BF16)
     du = hand_over(wu, yh, au)
-    arrive(r_wm)
     for j in range(4):
         pltpu.make_async_copy(cst, cz.at[j], jsem.at[4 + j]).wait()
 
     wmod = wm[...].reshape(384, 1152)
     pooled = cz[...].reshape(128, 384)
-    mps[...] = dot_nn(pooled, wmod).astype(BF16).reshape(4, rows, 1152)
-    r_mr = []
+    mps[...] = dot_nn(pooled, wmod[:, :768]).astype(BF16).reshape(4, rows, 768)
+    r_mr, r_mg = [], []
     for d in (2, 1, 3):
         dev = zdev(2 * d)
         r_mr.append(send(mps.at[dev[1] // 2], mrs.at[d - 1], dev))
-    mod = mps[pair].astype(F32)
+    mpg[...] = dot_nn(pooled, wmod[:, 768:]).astype(BF16).reshape(4, rows, 384)
+    for d in (2, 1, 3):
+        dev = zdev(2 * d)
+        r_mg.append(send(mpg.at[dev[1] // 2], mrg.at[d - 1], dev))
     arrive([y_wu])
+    y_wd = send(half(w_down, 1 - yh), own_d, pdev(4))
     cu = to_neighbours(oth_u, oth_u)
     ad = to_neighbours(half(w_down, yh), own_d)
+
+    def to_group(which, val):
+        slot[which] = dot_nn(onehot, val).astype(BF16).reshape(8, 16, 384)
+        hd[which, m, pl.ds(0, 16)] = slot[which, z]
+        out = []
+        for d in (4, 3, 5, 2, 6, 1, 7):
+            dev = zdev(d)
+            out.append(send(slot.at[which, dev[1]], hd.at[which, m, pl.ds(16 * d, 16)], dev))
+        return out
+
+    mod = mps[pair].astype(F32)
     arrive(r_mr)
     for d in range(3):
         mod = mod + mrs[d].astype(F32)
-    shift, scale, gate = mod[:, :384], mod[:, 384:768], mod[:, 768:]
-
-    h_in = (normed * (1.0 + scale) + shift).astype(BF16)
-    d_out = (gate * cot).astype(BF16)
-    packed = dot_nn(onehot, jnp.concatenate([h_in, d_out], axis=1)).astype(BF16)
-    slot[...] = packed.reshape(8, 16, 768)
-    r_sl = []
-    for d in (4, 3, 5, 2, 6, 1, 7):
-        dev = zdev(d)
-        r_sl.append(send(slot.at[dev[1]], hd.at[m, pl.ds(16 * d, 16)], dev))
-    hd[m, pl.ds(0, 16)] = slot[z]
-    arrive(r_sl)
-
-    def piece(k, lo):
-        return hd.at[k, :, pl.ds(lo, 384)]
-
-    first = []
-    for lo in (0, 384):
-        first.append([send(piece(m, lo), piece(m, lo), ydev(d)) for d in (2, 1, 3)])
-    eu = hand_over(wu, 1 - yh, cu)
+    r_sh = to_group(0, (normed * (1.0 + mod[:, 384:]) + mod[:, :384]).astype(BF16))
+    gate = mpg[pair].astype(F32)
+    arrive(r_mg)
+    for d in range(3):
+        gate = gate + mrg[d].astype(F32)
+    r_sd = to_group(1, (gate * cot).astype(BF16))
+
+    first, second = [], []
+    for which, got in ((0, r_sh), (1, r_sd)):
+        arrive(got)
+        here_rows = hd.at[which, m]
+        first.append([send(here_rows, here_rows, ydev(d)) for d in (2, 1, 3)])
+        second.append([send(here_rows, here_rows, twin)])
+        if which == 0:
+            eu = hand_over(wu, 1 - yh, cu)
     arrive([y_wd])
     cd = to_neighbours(oth_d, oth_d)
     dd = hand_over(wd, yh, ad)
-    second = [[send(piece(m, lo), piece(m, lo), twin)] for lo in (0, 384)]
     r_pk += [send(pick, pkg.at[par * 4 + pair], zdev(d)) for d in (4, 3, 5, 2, 6)]
 
-    def hand_on(which, lo):
+    def hand_on(which):
         for c, d in zip(first[which], (2, 1, 3)):
             arrive([c])
             k = 2 * lax.rem(ypos + 4 - d, 4) + core
-            second[which].append(send(piece(k, lo), piece(k, lo), twin))
-
-    hand_on(0, 0)
+            second[which].append(send(hd.at[which, k], hd.at[which, k], twin))
+
+    hand_on(0)
     arrive(second[0])
     c_wu.wait()
     arrive(du + eu)
 
-    def both(k, lo):
-        return jnp.concatenate([hd[k, :, lo : lo + 384], hd[4 + k, :, lo : lo + 384]], axis=0)
+    def both(which, k):
+        return jnp.concatenate([hd[which, k], hd[which, 4 + k]], axis=0)
 
     def reduce_out(val, weight, out, sib, whole, got):
         for k in range(4):
@@ -331,57 +347,72 @@
 
     pre = dot_nn(both(0, 0), wu[0:384, :])
     for k in range(1, 4):
-        pre = pre + dot_nn(both(k, 0), wu[384 * k : 384 * k + 384, :])
+        pre = pre + dot_nn(both(0, k), wu[384 * k : 384 * k + 384, :])
     value, slope = gelu_pair(pre)
     act = value.astype(BF16)
     slope_s[...] = slope
-    hand_on(1, 384)
+    hand_on(1)
     c_wd.wait()
     ed = hand_over(wd, 1 - yh, cd)
     arrive(dd + ed)
     ff_ex = reduce_out(act, wd, ffs, fsib, fsum, rff)
     arrive(second[1])
-    d_act = dot_nn(both(0, 384), wd[0:384, :])
+    d_act = dot_nn(both(1, 0), wd[0:384, :])
     for k in range(1, 4):
-        d_act = d_act + dot_nn(both(k, 384), wd[384 * k : 384 * k + 384, :])
+        d_act = d_act + dot_nn(both(1, k), wd[384 * k : 384 * k + 384, :])
     d_pre = (d_act * slope_s[...]).astype(BF16)
     r_ff = reduce_chips(ff_ex, ffs, fsib, fsum, rff)
     dh_ex = reduce_out(d_pre, wu, dhs, dsib, dsum, rdh)
     r_dh = reduce_chips(dh_ex, dhs, dsib, dsum, rdh)
-    rets[:, :, pl.ds(0, 384)] = reduce_end(r_ff, fsum, rff)
-    rets[:, :, pl.ds(384, 384)] = reduce_end(r_dh, dsum, rdh)
-    r_rt = [send(rets.at[d], ret.at[z], zdev(-d)) for d in (4, 3, 5, 2, 6, 1, 7)]
-    ret[z] = rets[0]
+    rets[0] = reduce_end(r_ff, fsum, rff)
+    r_rt = [send(rets.at[0, d], ret.at[0, z], zdev(-d)) for d in (4, 3, 5, 2, 6, 1, 7)]
+    ret[0, z] = rets[0, 0]
+    rets[1] = reduce_end(r_dh, dsum, rdh)
+    r_rd = [send(rets.at[1, d], ret.at[1, z], zdev(-d)) for d in (4, 3, 5, 2, 6, 1, 7)]
+    ret[1, z] = rets[1, 0]
     arrive(r_rt)
-    home = dot_nn(onehot_f, ret[...].reshape(128, 768))
-    ff_out, d_hin = home[:, :384], home[:, 384:]
-    d_mod = jnp.concatenate(
-        [valid * d_hin, valid * (d_hin * normed), valid * (cot * ff_out)], axis=1
-    )
-    rdm[pair] = d_mod.astype(BF16)
-    r_dm = [send(rdm.at[pair], rdm.at[pair], zdev(2 * d)) for d in (2, 1, 3)]
+    ff_out = dot_nn(onehot_f, ret[0].reshape(128, 384))
+    rdm2[pair] = (valid * (cot * ff_out)).astype(BF16)
+    r_dm = [send(rdm2.at[pair], rdm2.at[pair], zdev(2 * d)) for d in (2, 1, 3)]
     gen_o[...] = (valid * (lat_t + gate * ff_out)).reshape(4, 8, 384).astype(BF16)
+    arrive(r_rd)
+    d_hin = dot_nn(onehot_f, ret[1].reshape(128, 384))
+    rdm[pair] = jnp.concatenate([valid * d_hin, valid * (d_hin * normed)], axis=1).astype(BF16)
+    r_dn = [send(rdm.at[pair], rdm.at[pair], zdev(2 * d)) for d in (2, 1, 3)]
     arrive(r_dm)
-    dcs[...] = dot_nt(rdm[...].reshape(128, 1152), wm[...].reshape(384, 1152)).astype(BF16)
-    r_dc = [send(dcs, dcr.at[e - 1], tdev(e)) for e in (2, 3, 1)]
-    arrive(r_dc)
-    d_cond = dcs[...].astype(F32)
-    for e in range(3):
-        d_cond = d_cond + dcr[e].astype(F32)
-    d_cond = d_cond.astype(BF16)
-    turned = d_cond.astype(F32).T
+    wmod = wm[...].reshape(384, 1152)
+    dc_part = dot_nt(rdm2[...].reshape(128, 384), wmod[:, 768:])
+    arrive(r_dn)
+    dc_part = dc_part + dot_nt(rdm[...].reshape(128, 768), wmod[:, :768])
+    turned = dc_part.T
     for h in range(2):
-        dcx[h] = jnp.concatenate(
+        dcs[h] = jnp.concatenate(
             [turned[48 * pp + 24 * h : 48 * pp + 24 * h + 24] for pp in range(8)], axis=0
         ).astype(BF16)
+
+    def over_tp(h):
+        return [send(dcs.at[h], dcr.at[h, e - 1], tdev(e)) for e in (2, 3, 1)]
+
+    def summed(h, copies):
+        arrive(copies)
+        res = dcs[h].astype(F32)
+        for e in range(3):
+            res = res + dcr[h, e].astype(F32)
+        dcx[h] = res.astype(BF16)
+
+    r_d1 = over_tp(1 - par)
+    r_d0 = over_tp(par)
+    summed(1 - par, r_d1)
     r_df = [send(dcx.at[1 - par], dcf.at[par], partner)]
-    dcz[...] = d_cond.reshape(4, rows, 384)
+    summed(par, r_d0)
+    dcf[par] = dcx[par]
+    d_cond = jnp.concatenate([dcx[0].astype(F32), dcx[1].astype(F32)], axis=0).T
+    dcz[...] = d_cond.astype(BF16).reshape(4, rows, 384)
     r_dz = []
     for d in (2, 1, 3):
         dev = zdev(2 * d)
         r_dz.append(send(dcz.at[dev[1] // 2], dch.at[pair], dev))
     dch[pair] = dcz[pair]
-    dcf[par] = dcx[par]
 
     arrive(r_pk)
     arrive(r_df)
@@ -405,7 +436,9 @@
     pieces = []
     for pp in range(8):
         for q in range(4):
-            pieces.append(back[384 * q + 48 * pp : 384 * q + 48 * pp + 48])
+            for h in range(2):
+                k = 384 * q + 192 * h + 24 * pp
+                pieces.append(back[k : k + 24])
     back = jnp.concatenate(pieces, axis=0).T.astype(BF16)
     for i in range(4):
         cols = pl.ds(512 * i, 512)
@@ -442,7 +475,7 @@
     sm = pl.BlockSpec(memory_space=pltpu.SMEM)
     hb = pl.BlockSpec(memory_space=pl.ANY)
     V = pltpu.VMEM
-    n_copies = 144
+    n_copies = 200
     outs = pl.pallas_call(
         kernel,
         out_shape=(
@@ -460,7 +493,7 @@
             V((1536, 2048), BF16),
             V((1536, 768), BF16),
             V((1536, 768), BF16),
-            V((2, 32, 1152), BF16),
+            V((2, 8, 24, 1152), BF16),
             V((8, 48, 1152), BF16),
             V((32, 2048), BF16),
             V((8, 32, 2048), BF16),
@@ -468,10 +501,12 @@
             V((3, 32, 384), BF16),
             V((32, 384), BF16),
             V((4, 32, 384), BF16),
-            V((4, 32, 1152), BF16),
-            V((3, 32, 1152), BF16),
-            V((8, 16, 768), BF16),
-            V((8, 128, 768), BF16),
+            V((4, 32, 768), BF16),
+            V((3, 32, 768), BF16),
+            V((4, 32, 384), BF16),
+            V((3, 32, 384), BF16),
+            V((2, 8, 16, 384), BF16),
+            V((2, 8, 128, 384), BF16),
             V((256, 768), F32),
             V((2, 4, 128, 384), BF16),
             V((4, 128, 384), BF16),
@@ -481,11 +516,12 @@
             V((4, 128, 384), BF16),
             V((4, 128, 384), BF16),
             V((3, 128, 384), BF16),
-            V((8, 16, 768), BF16),
-            V((8, 16, 768), BF16),
-            V((4, 32, 1152), BF16),
-            V((128, 384), BF16),
-            V((3, 128, 384), BF16),
+            V((2, 8, 16, 384), BF16),
+            V((2, 8, 16, 384), BF16),
+            V((4, 32, 768), BF16),
+            V((4, 32, 384), BF16),
+            V((2, 192, 128), BF16),
+            V((2, 3, 192, 128), BF16),
             V((4, 32, 384), BF16),
             V((2, 192, 128), BF16),
             V((2, 192, 128), BF16),

time: 125 us -> 116 us (0.928)
  Pallas kernels: 125 us -> 115 us
    pallas_call x1, Pallas kernels: 123 us -> 113 us  [local(): pl.pallas_call(kernel, out_shape=(jax.ShapeDtypeStruct((4, 8, 384), BF16)...]
where the time goes in v3:
time: 116 us
  Pallas kernels  115 us (99%)
    pallas_call x1, Pallas kernels, local(): pl.pallas_call(kernel, out_shape=(jax.ShapeDtypeStruct((4, 8, 384), BF16)...  113 us

profile of v3, /device:TPU:1, one launch (start us, length us, event | category | flops | bytes accessed | tf_op | source)
XLA Modules:
  0.0 115.6 jit_solution(12784091253025414733)
XLA Ops:
  0.6 113.2 %shard_map.121 = (bf16[4,8,384]{2,1,0:T(8,128)(2,1)}, bf16[4,8,2048]{2,1,0:T(8,128)(2,1)}, f32[24,2048]{1,0:T(8,128)}) custom-call(s32[4]{0:T(128)} %bitcast.3, s32[4]{0:T(128)} %tokens.1, s32[4,8]{1,0:T(4,128)} %positions.1, bf16[4,128,2048]{2,1,0:T(8,128)(2,1)} %hidden.1, bf16[4,8,1536]{2,1,0:T(8,128)(2,1)} %latents_h.1, bf16[4,8,384]{2,1,0:T(8,128)(2,1)} %out_grad_h.1, ...), custom_call_target="tpu_custom_call" | custom-call | flops 6000000000 | bytes 16000000 | tf_op jit(solution)/shard_map/pallas_call | solution.py:479
  113.8 1.7 %shard_map.122 = (bf16[4,8,384]{2,1,0:T(8,128)(2,1)}, bf16[4,8,2048]{2,1,0:T(8,128)(2,1)}, f32[24,2048]{1,0:T(8,128)}) custom-call(bf16[4,8,384]{2,1,0:T(8,128)(2,1)} %get-tuple-element.6.gen, bf16[4,8,2048]{2,1,0:T(8,128)(2,1)} %get-tuple-element.7.row, f32[24,2048]{1,0:T(8,128)} %get-tuple-element.8.conn), custom_call_target="tpu_custom_call" | custom-call | tf_op jit(solution)/shard_map/pallas_call | solution.py:546

commit v4 on v3

--- a/solution.py
+++ b/solution.py
@@ -330,13 +330,19 @@
             res = dot_nt(val, weight[384 * k : 384 * k + 384, :]).astype(BF16)
             out[k % 2, k // 2] = res[:128]
             out[k % 2, 2 + k // 2] = res[128:]
-        return [send(out.at[1 - core, d], sib.at[d], twin) for d in range(4)]
+        return [
+            send(out.at[1 - core, yplace(d)], sib.at[yplace(d)], twin) for d in (2, 1, 3, 0)
+        ]
 
     def reduce_chips(ex, out, sib, whole, got):
-        arrive(ex)
-        for d in range(4):
-            whole[d] = (out[core, d].astype(F32) + sib[d].astype(F32)).astype(BF16)
-        return [send(whole.at[yplace(d)], got.at[d - 1], ydev(d)) for d in (2, 1, 3)]
+        sends = []
+        for c, d in zip(ex, (2, 1, 3, 0)):
+            arrive([c])
+            k = yplace(d)
+            whole[k] = (out[core, k].astype(F32) + sib[k].astype(F32)).astype(BF16)
+            if d > 0:
+                sends.append(send(whole.at[k], got.at[d - 1], ydev(d)))
+        return sends
 
     def reduce_end(ex, whole, got):
         arrive(ex)

time: 116 us -> 115 us (level)
  no operation moved by 1% of the time
where the time goes in v4:
time: 115 us
  Pallas kernels  115 us (100%)
    pallas_call x1, Pallas kernels, local(): pl.pallas_call(kernel, out_shape=(jax.ShapeDtypeStruct((4, 8, 384), BF16)...  113 us

profile of v4, /device:TPU:1, one launch (start us, length us, event | category | flops | bytes accessed | tf_op | source)
XLA Modules:
  0.0 115.3 jit_solution(3759772434047271194)
XLA Ops:
  0.6 112.9 %shard_map.121 = (bf16[4,8,384]{2,1,0:T(8,128)(2,1)}, bf16[4,8,2048]{2,1,0:T(8,128)(2,1)}, f32[24,2048]{1,0:T(8,128)}) custom-call(s32[4]{0:T(128)} %bitcast.3, s32[4]{0:T(128)} %tokens.1, s32[4,8]{1,0:T(4,128)} %positions.1, bf16[4,128,2048]{2,1,0:T(8,128)(2,1)} %hidden.1, bf16[4,8,1536]{2,1,0:T(8,128)(2,1)} %latents_h.1, bf16[4,8,384]{2,1,0:T(8,128)(2,1)} %out_grad_h.1, ...), custom_call_target="tpu_custom_call" | custom-call | flops 6000000000 | bytes 16000000 | tf_op jit(solution)/shard_map/pallas_call | solution.py:485
  113.5 1.7 %shard_map.122 = (bf16[4,8,384]{2,1,0:T(8,128)(2,1)}, bf16[4,8,2048]{2,1,0:T(8,128)(2,1)}, f32[24,2048]{1,0:T(8,128)}) custom-call(bf16[4,8,384]{2,1,0:T(8,128)(2,1)} %get-tuple-element.6.gen, bf16[4,8,2048]{2,1,0:T(8,128)(2,1)} %get-tuple-element.7.row, f32[24,2048]{1,0:T(8,128)} %get-tuple-element.8.conn), custom_call_target="tpu_custom_call" | custom-call | tf_op jit(solution)/shard_map/pallas_call | solution.py:552
